TPU v7x, 256 devices: a whole 4x4x8 slice. The times are simulated.
256 devices in a mesh: section: 8 (over x, core), tensor: 32 (over z, y).
Axes of the slice: x: 4, y: 4, z: 8, core: 2. Of those that a mesh axis runs over, the one named last changes fastest.
Arguments:
- layer_input: bfloat16 [8, 256, 8192], P('section', None, 'tensor'), may hold values from -6 to 6
- upstream: bfloat16 [8, 256, 8192], P('section', None, 'tensor'), may hold values from -6 to 6
- query_rows: bfloat16 [8, 256, 8192], P('section', None, 'tensor'), may hold values from -4.5 to 4.5
- key_rows: bfloat16 [8, 256, 8192], P('section', None, 'tensor'), may hold values from -4.5 to 4.5
- norm_gain: bfloat16 [8, 8192], P('section'), may hold values from 0.5 to 1.5
- out_tiles: bfloat16 [8, 10240, 4096], P('section', 'tensor'), may hold values from -0.09375 to 0.09375
- out_ids: int32 [8, 10240], P('section', 'tensor'), may hold values from 0 to 511, as said below
- out_count: int32 [8, 32], P('section', 'tensor'), may hold values from 192 to 320, as said below
- value_tiles: bfloat16 [8, 10240, 4096], P('section', 'tensor'), may hold values from -0.09375 to 0.09375
- value_ids: int32 [8, 10240], P('section', 'tensor'), may hold values from 0 to 511, as said below
- value_count: int32 [8, 32], P('section', 'tensor'), may hold values from 192 to 320, as said below
Outputs:
- grad_input: bfloat16 [8, 256, 8192], P('section', None, 'tensor')
- out_grad: bfloat16 [8, 10240, 4096], P('section', 'tensor')
- value_grad: bfloat16 [8, 10240, 4096], P('section', 'tensor')
Inputs may be any that keep to these rules, and one draw needn't show every extreme that they name: `out_ids`: within each shard's 320 slots the tile numbers are distinct; slots at or after the shard's count are not stored tiles. `out_count`: in every section some shard holds exactly 320 stored tiles. `value_ids`: within each shard's 320 slots the tile numbers are distinct; slots at or after the shard's count are not stored tiles. `value_count`: in every section some shard holds exactly 320 stored tiles.
All inputs are finite; a program needn't handle non-finite values.
Results may differ from a plain program's by a relative error of at most 0.0085.
Values may be sent and summed in bfloat16 or wider, within the bound.
A program may use at most 128 MiB of HBM per device.

v0:
```python
import jax
import jax.numpy as jnp
from jax import lax
from jax.sharding import PartitionSpec as P

HEAD = 128
EDGE = 64


EPS = 1e-05


def passed_along(block, axis, distance):
    devices = range(lax.axis_size(axis))
    route = [(i - distance, i) for i in devices if i - distance in devices]
    return lax.ppermute(block, axis, route)


def group_length(slot_count):
    group_len = 64
    while slot_count % group_len:
        group_len = group_len // 2
    return group_len


def select_blocks(blocked, indices, block_total):
    selector = (indices[:, None] == jnp.arange(block_total, dtype=jnp.int32)[None, :]).astype(
        blocked.dtype
    )
    picked = jnp.einsum("tck,gc->tgk", blocked, selector, preferred_element_type=jnp.float32)
    return picked.astype(blocked.dtype)


def live_tiles(blocks, numbers, filled, start_slot, group_len):
    tile_block = lax.dynamic_slice_in_dim(blocks, start_slot, group_len, 0).reshape(
        group_len, EDGE, EDGE
    )
    numbers_now = lax.dynamic_slice_in_dim(numbers, start_slot, group_len, 0)
    present = start_slot + jnp.arange(group_len, dtype=jnp.int32) < filled
    tile_block = jnp.where(present[:, None, None], tile_block, jnp.zeros((), tile_block.dtype))
    return (tile_block, numbers_now)


def sparse_product(source, blocks, numbers, filled, col_blocks, out_blocks, pattern):
    row_count = source.shape[0]
    blocked = source.reshape(row_count, -1, EDGE)
    group_len = group_length(blocks.shape[0])

    def sparse_one_group(iteration, accumulated):
        start_slot = iteration * group_len
        tile_block, numbers_now = live_tiles(blocks, numbers, filled, start_slot, group_len)
        gathered = select_blocks(blocked, numbers_now % col_blocks, col_blocks)
        products = jnp.einsum(pattern, gathered, tile_block, preferred_element_type=jnp.float32)
        placer = (
            (numbers_now // col_blocks)[:, None] == jnp.arange(out_blocks, dtype=jnp.int32)[None, :]
        ).astype(jnp.float32)
        return accumulated + jnp.einsum(
            "gtj,go->otj", products, placer, precision=lax.Precision.HIGHEST
        )

    accumulated = jnp.zeros((out_blocks, row_count, EDGE), jnp.float32)
    accumulated = lax.fori_loop(
        0, (filled + group_len - 1) // group_len, sparse_one_group, accumulated
    )
    return jnp.transpose(accumulated, (1, 0, 2)).reshape(row_count, out_blocks * EDGE)


def tile_gradient(left_data, right_data, numbers, filled, col_blocks, left_rows):
    row_count = left_data.shape[0]
    left_blocked = left_data.reshape(row_count, -1, EDGE)
    right_blocked = right_data.reshape(row_count, -1, EDGE)
    left_total = left_blocked.shape[1]
    right_total = right_blocked.shape[1]
    slot_count = numbers.shape[0]
    group_len = group_length(slot_count)

    def tile_one_group(iteration, gradients):
        start_slot = iteration * group_len
        numbers_now = lax.dynamic_slice_in_dim(numbers, start_slot, group_len, 0)
        present = start_slot + jnp.arange(group_len, dtype=jnp.int32) < filled
        if left_rows:
            left_blocks, right_blocks = (numbers_now // col_blocks, numbers_now % col_blocks)
        else:
            left_blocks, right_blocks = (numbers_now % col_blocks, numbers_now // col_blocks)
        gradient = jnp.einsum(
            "tgi,tgj->gij",
            select_blocks(left_blocked, left_blocks, left_total),
            select_blocks(right_blocked, right_blocks, right_total),
            preferred_element_type=jnp.float32,
        )
        gradient = jnp.where(present[:, None, None], gradient, 0.0).astype(jnp.bfloat16)
        return lax.dynamic_update_slice_in_dim(
            gradients, gradient.reshape(group_len, EDGE * EDGE), start_slot, 0
        )

    gradients = jnp.zeros((slot_count, EDGE * EDGE), jnp.bfloat16)
    return lax.fori_loop(0, (filled + group_len - 1) // group_len, tile_one_group, gradients)


def dense_grid(blocks, numbers, filled, row_blocks, col_blocks):
    slot_count = blocks.shape[0]
    present = jnp.arange(slot_count, dtype=jnp.int32) < filled
    positions = jnp.arange(row_blocks * col_blocks, dtype=jnp.int32)
    placer = ((numbers[:, None] == positions[None, :]) & present[:, None]).astype(blocks.dtype)
    grid_data = jnp.einsum("sp,sq->pq", placer, blocks, preferred_element_type=jnp.float32)
    return grid_data.astype(blocks.dtype).reshape(row_blocks, col_blocks, EDGE, EDGE)


def attend(queries, keyset, values, mixed_grad, head_count):
    tokens = queries.shape[0]
    query_heads = queries.reshape(tokens, head_count, HEAD)
    key_heads = keyset.reshape(tokens, head_count, HEAD)
    value_heads = values.reshape(tokens, head_count, HEAD)
    grad_heads = mixed_grad.reshape(tokens, head_count, HEAD)
    scores = jnp.einsum(
        "thd,shd->hts", query_heads, key_heads, preferred_element_type=jnp.float32
    ) * HEAD ** (-0.5)
    causal = jnp.arange(tokens)[:, None] >= jnp.arange(tokens)[None, :]
    scores = jnp.where(causal[None], scores, -1e30)
    row_max = jnp.max(scores, axis=-1, keepdims=True)
    weights = jnp.exp(scores - row_max)
    probabilities = (weights / jnp.sum(weights, axis=-1, keepdims=True)).astype(jnp.bfloat16)
    attended = jnp.einsum(
        "hts,shd->thd", probabilities, value_heads, preferred_element_type=jnp.float32
    )
    value_grads = jnp.einsum(
        "hts,thd->shd", probabilities, grad_heads, preferred_element_type=jnp.float32
    )
    local_width = queries.shape[1]
    return (
        attended.astype(jnp.bfloat16).reshape(tokens, local_width),
        value_grads.astype(jnp.bfloat16).reshape(tokens, local_width),
    )


def per_device(
    layer_input,
    upstream,
    query_rows,
    key_rows,
    norm_gain,
    out_tiles,
    out_ids,
    out_count,
    value_tiles,
    value_ids,
    value_count,
):
    rows_here = layer_input[0]
    grads_here = upstream[0]
    queries = query_rows[0]
    keyset = key_rows[0]
    gain_row = norm_gain[0]
    out_blocks = out_tiles[0]
    out_numbers = out_ids[0]
    out_filled = out_count[0, 0]
    value_blocks = value_tiles[0]
    value_numbers = value_ids[0]
    value_filled = value_count[0, 0]
    local_width = queries.shape[1]
    model_width = gain_row.shape[0]
    col_blocks = model_width // EDGE
    row_blocks = local_width // EDGE
    head_count = local_width // HEAD
    wide = rows_here.astype(jnp.float32)
    squares = lax.psum(jnp.sum(wide * wide, axis=-1, keepdims=True), "tensor")
    inverse_rms = lax.rsqrt(squares / model_width + EPS)
    gain_local = lax.dynamic_slice_in_dim(
        gain_row, lax.axis_index("tensor") * local_width, local_width, 0
    )
    normed_here = (wide * inverse_rms * gain_local.astype(jnp.float32)).astype(jnp.bfloat16)
    normed_all, upstream_all = (
        lax.all_gather(normed_here, "tensor", axis=1, tiled=True),
        lax.all_gather(grads_here, "tensor", axis=1, tiled=True),
    )
    value_grid = dense_grid(value_blocks, value_numbers, value_filled, row_blocks, col_blocks)
    value_dense = value_grid.transpose(1, 2, 0, 3).reshape(model_width, local_width)
    values = sparse_product(
        normed_all,
        value_blocks,
        value_numbers,
        value_filled,
        col_blocks,
        row_blocks,
        "tgk,gkj->gtj",
    )
    mixed_grad = sparse_product(
        upstream_all, out_blocks, out_numbers, out_filled, col_blocks, row_blocks, "tgk,gjk->gtj"
    )
    values = values.astype(jnp.bfloat16)
    mixed_grad = mixed_grad.astype(jnp.bfloat16)
    attended, value_grads = attend(queries, keyset, values, mixed_grad, head_count)
    partial_terms = jnp.dot(value_grads, value_dense.T, preferred_element_type=jnp.float32)
    summed = lax.psum_scatter(
        partial_terms.astype(jnp.bfloat16), "tensor", scatter_dimension=1, tiled=True
    ).astype(jnp.float32)
    section_grad = (grads_here.astype(jnp.float32) + summed).astype(jnp.bfloat16)
    passed = passed_along(section_grad, "section", -1)
    out_grad = tile_gradient(attended, upstream_all, out_numbers, out_filled, col_blocks, True)
    value_grad = tile_gradient(
        normed_all, value_grads, value_numbers, value_filled, col_blocks, False
    )
    return (passed[None], out_grad[None], value_grad[None])


def solution(mesh):
    return jax.shard_map(
        per_device,
        mesh=mesh,
        in_specs=(
            P("section", None, "tensor"),
            P("section", None, "tensor"),
            P("section", None, "tensor"),
            P("section", None, "tensor"),
            P("section", None),
            P("section", "tensor", None),
            P("section", "tensor"),
            P("section", "tensor"),
            P("section", "tensor", None),
            P("section", "tensor"),
            P("section", "tensor"),
        ),
        out_specs=(
            P("section", None, "tensor"),
            P("section", "tensor", None),
            P("section", "tensor", None),
        ),
        check_vma=False,
    )
```

profile of v0, /device:TPU:1, one launch (start us, length us, event | category | flops | bytes accessed | tf_op | source)
XLA Modules:
  0.0 602.8 jit_solution(10786115756905269501)
XLA Ops:
  8.3 64.6 %psum.7 = f32[256,1]{0,1:T(1,128)S(1)} all-reduce(f32[256,1]{0,1:T(1,128)S(1)} %bitcast.146), channel_id=1, replica_groups=mesh['section'=8,'tensor'=32] {'tensor'}, use_global_device_ids=true, to_apply=%region_6.7 | all-reduce | flops 256 | bytes 2048 | tf_op jit(solution)/shard_map/psum | solution.py:166
  80.7 6.2 %convolution_convert_fusion.1 = bf16[512,4096]{1,0:T(8,128)(2,1)} fusion(s32[320]{0:T(512)S(1)} %reduce.1, pred[320]{0:T(512)(128)(4,1)S(1)} %iota_compare_fusion.10, bf16[1,320,4096]{2,1,0:T(8,128)(2,1)} %param.27), kind=kOutput, calls=%fused_computation.86 | convolution fusion | flops 1344602112 | bytes 6817344 | tf_op jit(solution)/shard_map/sp,sq->pq/dot_general | solution.py:105
  86.9 6.5 %copy.75 = bf16[512,4096]{0,1:T(8,128)(2,1)} copy(bf16[512,4096]{1,0:T(8,128)(2,1)} %convolution_convert_fusion.1) | data formatting | bytes 8388608 | tf_op jit(solution)/shard_map/convert_element_type | solution.py:106
  93.4 7.0 %reshape.107 = bf16[4,128,64,64]{1,0,3,2:T(4,128)(2,1)} reshape(bf16[512,4096]{0,1:T(8,128)(2,1)} %copy.75) | data formatting | bytes 8388608 | tf_op jit(solution)/shard_map/reshape | solution.py:106
  100.4 10.3 %copy.76 = bf16[128,64,4,64]{1,0,3,2:T(8,128)(2,1)} copy(bf16[128,64,4,64]{0,2,3,1:T(4,128)(2,1)} %bitcast.131) | data formatting | bytes 8388608 | tf_op jit(solution)/shard_map/transpose | solution.py:177
  110.7 12.1 %reshape.108 = bf16[8192,256]{0,1:T(8,128)(2,1)} reshape(bf16[128,64,4,64]{1,0,3,2:T(8,128)(2,1)} %copy.76) | data formatting | bytes 8388608 | tf_op jit(solution)/shard_map/reshape | solution.py:177
  123.1 39.4 %all-gather.4.cloned.1.call-done = bf16[256,8192]{0,1:T(8,128)(2,1)} async-done(((bf16[256,256]{0,1:T(8,128)(2,1)}), bf16[256,8192]{0,1:T(8,128)(2,1)}) %all-gather.4.cloned.1.call-update) | async-done | bytes 4194320 | tf_op jit(solution)/shard_map/all_gather | solution.py:173
  162.5 6.9 %copy.78 = bf16[256,128,64]{1,0,2:T(8,128)(2,1)} copy(bf16[256,128,64]{0,2,1:T(8,128)(2,1)} %bitcast.132) | data formatting | bytes 8388608 | tf_op jit(solution)/shard_map/while | solution.py:62
  169.3 75.4 %all-gather.6.cloned.1.call-done = bf16[1,256,8192]{1,2,0:T(8,128)(2,1)} async-done(((bf16[1,256,256]{1,2,0:T(8,128)(2,1)}), bf16[1,256,8192]{1,2,0:T(8,128)(2,1)}) %all-gather.6.cloned.1.call-update) | async-done | bytes 4194320 | tf_op jit(solution)/shard_map/all_gather | solution.py:174
  244.8 6.8 %copy.70 = bf16[256,128,64]{1,0,2:T(8,128)(2,1)} copy(bf16[256,128,64]{0,2,1:T(8,128)(2,1)} %bitcast.133) | data formatting | bytes 8388608 | tf_op jit(solution)/shard_map/while | solution.py:62
  251.6 62.4 %while.48 = (s32[]{:T(128)}, f32[4,256,64]{1,0,2:T(4,128)S(1)}, s32[]{:T(128)}, s32[320]{0:T(512)S(1)}, bf16[256,128,64]{1,0,2:T(8,128)(2,1)}, /*index=5*/s32[]{...) while((s32[]{:T(128)}, f32[4,256,64]{1,0,2:T(4,128)S(1)}, ...), condition=%wide.region_1.0_spmd, body=%wide.region_0.0_spmd.sunk | while | flops 454370944 | bytes 19925036 | solution.py:62
  260.3 3.9 fusion.152
  272.7 3.9 fusion.152
  285.2 3.9 fusion.152
  297.6 3.9 fusion.152
  310.0 3.9 fusion.152
  314.6 5.4 convolution_convert_fusion
  320.1 63.3 %while.49 = (s32[]{:T(128)}, f32[4,256,64]{1,0,2:T(4,128)S(1)}, s32[]{:T(128)}, s32[320]{0:T(512)S(1)}, bf16[256,128,64]{1,0,2:T(8,128)(2,1)}, /*index=5*/s32[]{...) while((s32[]{:T(128)}, f32[4,256,64]{1,0,2:T(4,128)S(1)}, ...), condition=%wide.region_8.9_spmd, body=%wide.region_7.8_spmd.sunk | while | flops 454370944 | bytes 19925036 | solution.py:62
  329.0 3.9 fusion.160
  341.6 3.9 fusion.160
  386.0 47.6 %while.50 = (s32[]{:T(128)}, bf16[320,4096]{1,0:T(8,128)(2,1)}, s32[]{:T(128)}, s32[]{:T(128)}, s32[320]{0:T(512)S(1)}, /*index=5*/bf16[256,4,64]{0,1,2:T(4,128)...) while((s32[]{:T(128)}, bf16[320,4096]{1,0:T(8,128)(2,1)}, ...), condition=%wide.region_10.11_spmd, body=%wide.region_9.10_spmd.sunk | while | flops 413673088 | bytes 15337515 | solution.py:97
  433.5 103.7 %reduce-scatter.2.cloned.1.call-done = bf16[256,256]{1,0:T(8,128)(2,1)} async-done(((bf16[256,8192]{1,0:T(8,128)(2,1)}), bf16[256,256]{1,0:T(8,128)(2,1)}) %reduce-scatter.2.cloned.1.call-update) | async-done | bytes 131088 | tf_op jit(solution)/shard_map/reduce_scatter | solution.py:194
  538.2 7.8 %collective-permute-start = (bf16[256,256]{1,0:T(8,128)(2,1)S(1)}, bf16[256,256]{1,0:T(8,128)(2,1)S(1)}, u32[]{:S(2)}, u32[]{:S(2)}) collective-permute-start(bf16[256,256]{1,0:T(8,128)(2,1)S(1)} %fusion.71), channel_id=1, source_target_pairs={{32,0},{64,32},{96,64},{128,96},{160,128},{192,160},{224,192},{33,... | collective-permute-start | bytes 393224 | tf_op jit(solution)/shard_map/ppermute | solution.py:16
  547.8 47.8 %while.51 = (s32[]{:T(128)}, bf16[320,4096]{1,0:T(8,128)(2,1)}, s32[]{:T(128)}, s32[]{:T(128)}, s32[320]{0:T(512)S(1)}, /*index=5*/bf16[256,128,64]{1,0,2:T(8,12...) while((s32[]{:T(128)}, bf16[320,4096]{1,0:T(8,128)(2,1)}, ...), condition=%wide.region_12.13_spmd, body=%wide.region_11.12_spmd.sunk | while | flops 413673280 | bytes 15337775 | solution.py:97
  (187 shorter events, 207.0 us)
Async XLA Ops:
  7.2 155.3 %all-gather.4.cloned.1.call-start = ((), (), s32[]{:S(2)}) async-start(), calls=%async_computation.2 | async-start | bytes 4325376 | tf_op jit(solution)/shard_map/all_gather | solution.py:173
  74.3 170.4 %all-gather.6.cloned.1.call-start = ((), (), s32[]{:S(2)}) async-start(), calls=%async_computation.3 | async-start | bytes 4325376 | tf_op jit(solution)/shard_map/all_gather | solution.py:174
  76.1 461.2 %reduce-scatter.2.cloned.1.call-start = ((), (), s32[]{:S(2)}) async-start(), calls=%async_computation.1 | async-start | bytes 4325376 | tf_op jit(solution)/shard_map/reduce_scatter | solution.py:194
  386.0 151.3 %copy-start = (bf16[1,256,256]{2,1,0:T(8,128)(2,1)S(1)}, bf16[1,256,256]{2,1,0:T(8,128)(2,1)}, u32[]{:S(2)}) copy-start(bf16[1,256,256]{2,1,0:T(8,128)(2,1)} %param.20) | copy-start | bytes 393220
  538.2 57.4 %collective-permute-start = (bf16[256,256]{1,0:T(8,128)(2,1)S(1)}, bf16[256,256]{1,0:T(8,128)(2,1)S(1)}, u32[]{:S(2)}, u32[]{:S(2)}) collective-permute-start(bf16[256,256]{1,0:T(8,128)(2,1)S(1)} %fusion.71), channel_id=1, source_target_pairs={{32,0},{64,32},{96,64},{128,96},{160,128},{192,160},{224,192},{33,... | collective-permute-start | bytes 393224 | tf_op jit(solution)/shard_map/ppermute | solution.py:16
Sparse Core Ops, SparseCore 0:
  74.4 87.9 all-gather.3
  165.6 79.0 all-gather.5
  320.2 217.0 reduce-scatter.1
where the time goes:
time: 606 us; the launch traced here: 603 us
  waiting for transfers between devices  219 us (36%)
  matrix products  179 us (30%)
  local copies, waits for them, and re-layouts  97.2 us (16%)
  blocking collectives  64.6 us (11%)
  other arithmetic  19.1 us (3%)
  between operations  15.2 us (3%)
  starting transfers between devices  7.91 us (1%)
    reduce_scatter x1, waiting for transfers between devices, per_device(): lax.psum_scatter(partial_terms.astype(jnp.bfloat16), 'tensor', scatter_di...  104 us
    dot_general x30, matrix products, select_blocks(): jnp.einsum('tck,gc->tgk', blocked, selector, preferred_element_type=jnp.f...  84 us
    all_gather x1, waiting for transfers between devices, per_device(): lax.all_gather(grads_here, 'tensor', axis=1, tiled=True)  75.4 us
    psum x1, blocking collectives, per_device(): squares = lax.psum(jnp.sum(wide * wide, axis=-1, keepdims=True), 'tensor')  64.6 us
    dot_general x10, matrix products, sparse_one_group(): jnp.einsum('gtj,go->otj', products, placer, precision=lax.Precision.HIGHEST)  39.4 us
    all_gather x1, waiting for transfers between devices, per_device(): lax.all_gather(normed_here, 'tensor', axis=1, tiled=True)  39.4 us
    dot_general x10, matrix products, tile_one_group(): jnp.einsum('tgi,tgj->gij', select_blocks(left_blocked, left_blocks, left_...  25 us
    dot_general x10, matrix products, sparse_one_group(): jnp.einsum(pattern, gathered, tile_block, preferred_element_type=jnp.floa...  17.8 us
  transfers between devices with their start and end apart: 4, of which 3 were waited for; matrix products, arithmetic and copies ran while one was open for 36% of the time, Pallas kernels for 0%

commit v1 on v0

v1 whole, which is shorter than its diff:
```python
import jax
import jax.numpy as jnp
from jax import lax
from jax.experimental import pallas as pl
from jax.experimental.pallas import tpu as pltpu
from jax.sharding import PartitionSpec as P

HEAD = 128
EDGE = 64
EPS = 1e-05
TOK = 256
WIDTH = 256
NZ = 8
NY = 4
CAP = 320
TILES = 512
COLS = 128
MODEL = 8192
HALF = EDGE // 2
CUT_U, CUT_X, CUT_P = 96, 112, 112
EXTRA = 16
BLOCKS = NZ * NY

BF = jnp.bfloat16
F32 = jnp.float32
NN = (((1,), (0,)), ((), ()))
NT = (((1,), (1,)), ((), ()))
TN = (((0,), (0,)), ((), ()))


def dot(a, b, dims=NN):
    return lax.dot_general(a, b, dims, preferred_element_type=F32)


class Links:
    def __init__(self, recv_sems):
        self.recv_sems = recv_sems
        self.used = 0
        place = lax.axis_index("tensor")
        self.place = place
        self.z, self.y = place // NY, place % NY
        self.to = {
            ("z", 1): self.at(1, 0),
            ("z", -1): self.at(-1, 0),
            ("y", 1): self.at(0, 1),
            ("y", -1): self.at(0, -1),
        }

    def at(self, dz, dy):
        return (self.z + (dz + NZ)) % NZ * NY + (self.y + (dy + NY)) % NY

    def semaphore(self):
        self.used += 1
        return self.recv_sems.at[self.used - 1]

    def send(self, src, dst, axis, way, send_sem, recv_sem):
        pltpu.make_async_remote_copy(
            src_ref=src,
            dst_ref=dst,
            send_sem=send_sem,
            recv_sem=recv_sem,
            device_id={"tensor": self.to[(axis, way)]},
            device_id_type=pl.DeviceIdType.MESH,
        ).start()


def wait_for(view, semaphore):
    pltpu.make_async_copy(view, view, semaphore).wait()


WAYS = (1, -1)


class Routes:
    def __init__(self, links, ref, rows, cut, send_sem):
        self.links, self.ref, self.send_sem = links, ref, send_sem
        self.a = (0, cut)
        first = cut // 32 * 16
        self.a_half = {1: (0, first), -1: (first, cut - first)}
        rest = rows - cut
        first = rest // 32 * 16
        self.b = (cut, rest)
        self.b_half = {1: (cut, first), -1: (cut + first, rest - first)}
        self.coming = {}

    def pair(self, key, axis, block, rows, halves, into=None):
        semaphore = self.links.semaphore()
        for way in WAYS:
            part = halves[way] if halves else rows
            src = self.ref.at[block(way), pl.ds(*part)]
            dst = src if into is None else into(way, part[1])
            self.links.send(src, dst, axis, way, self.send_sem, semaphore)
        if halves:
            view = self.ref.at[0, pl.ds(0, rows[1])]
        else:
            view = self.ref.at[pl.ds(0, 2), pl.ds(0, rows[1])]
        self.coming[key] = (view, semaphore)

    def wait(self, *key):
        wait_for(*self.coming.pop(key))

    def sent(self):
        wait_for(self.ref.at[pl.ds(0, BLOCKS - 1)], self.send_sem)


class Gather(Routes):
    def ay(self, step):
        at = self.links.at
        if step > 1:
            self.wait("ay", 1)
        self.pair(
            ("ay", step),
            "y",
            lambda way: at(0, -way * (step - 1)),
            self.a,
            self.a_half if step == 2 else None,
        )

    def az(self, step, *offsets):
        at = self.links.at
        for dy in offsets:
            if step > 1:
                self.wait("az", dy, step - 1)
            elif dy == 2:
                self.wait("ay", 2)
            self.pair(
                ("az", dy, step),
                "z",
                lambda way: at(-way * (step - 1), dy),
                self.a,
                self.a_half if step == 4 else None,
            )

    def bz(self, step):
        at = self.links.at
        if step > 1:
            self.wait("bz", step - 1)
        self.pair(
            ("bz", step),
            "z",
            lambda way: at(-way * (step - 1), 0),
            self.b,
            self.b_half if step == 4 else None,
        )

    def by1(self, *offsets):
        at = self.links.at
        for dz in offsets:
            if dz == 4:
                self.wait("bz", 4)
            self.pair(("by", dz, 1), "y", lambda way: at(dz, 0), self.b, None)

    def by2(self, *offsets):
        at = self.links.at
        for dz in offsets:
            self.wait("by", dz, 1)
            self.pair(("by", dz, 2), "y", lambda way: at(dz, -way), self.b, self.b_half)

    def begin(self):
        self.ay(1)
        self.bz(1)
        self.az(1, 0)
        self.by1(0)

    def steps(self):
        return [
            lambda: (self.ay(2), self.az(1, 1, -1)),
            lambda: (self.bz(2), self.by1(-1, 1)),
            lambda: self.az(2, 0),
            lambda: self.by2(0),
            lambda: self.az(1, 2),
            lambda: self.az(2, 1, -1),
            lambda: (self.bz(3), self.by1(-2, 2)),
            lambda: self.az(3, 0),
            lambda: self.by2(-1, 1),
            lambda: self.az(2, 2),
            lambda: self.az(3, 1, -1),
            lambda: (self.bz(4), self.by1(-3, 3)),
            lambda: self.az(4, 0),
            lambda: self.by2(-2, 2),
            lambda: self.az(3, 2),
            lambda: self.az(4, 1, -1),
            lambda: self.by1(4),
            lambda: self.by2(-3, 3),
            lambda: self.az(4, 2),
            lambda: self.by2(4),
            lambda: self.finish(),
        ]

    def finish(self):
        for key in sorted(self.coming):
            self.wait(*key)


class Scatter(Routes):
    def __init__(self, links, ref, cut, send_sem, az_in, by_in, ay_in, bz_in):
        super().__init__(links, ref, TOK, cut, send_sem)
        self.az_in, self.by_in, self.ay_in, self.bz_in = az_in, by_in, ay_in, bz_in

    def add(self, block, rows, *got):
        part = self.ref[block, pl.ds(*rows)].astype(F32)
        for more in got:
            part = part + more.astype(F32)
        self.ref[block, pl.ds(*rows)] = part.astype(BF)

    def az(self, step, *offsets):
        at = self.links.at
        for dy in offsets:
            if step > 1:
                self.wait("az", dy, step - 1)
                for way in WAYS:
                    rows = self.a if step > 2 else self.a_half[way]
                    got = self.az_in[(way + 1) // 2, step - 2, dy + 1, pl.ds(0, rows[1])]
                    self.add(at(way * (5 - step), dy), rows, got)
            self.pair(
                ("az", dy, step),
                "z",
                lambda way: at(way * (5 - step), dy),
                self.a,
                self.a_half if step == 1 else None,
                lambda way, size: self.az_in.at[(way + 1) // 2, step - 1, dy + 1, pl.ds(0, size)],
            )

    def az_done(self, *offsets):
        for dy in offsets:
            self.wait("az", dy, 4)
            self.add(self.links.at(0, dy), self.a, self.az_in[0, 3, dy + 1], self.az_in[1, 3, dy + 1])

    def by(self, step, *offsets):
        at = self.links.at
        for dz in offsets:
            if step > 1:
                self.wait("by", dz, 1)
                for way in WAYS:
                    rows = self.b_half[way]
                    got = self.by_in[(way + 1) // 2, 0, dz + 3, pl.ds(0, rows[1])]
                    self.add(at(dz, way), rows, got)
            self.pair(
                ("by", dz, step),
                "y",
                lambda way: at(dz, way * (3 - step)),
                self.b,
                self.b_half if step == 1 else None,
                lambda way, size: self.by_in.at[(way + 1) // 2, step - 1, dz + 3, pl.ds(0, size)],
            )

    def by_done(self, *offsets):
        for dz in offsets:
            self.wait("by", dz, 2)
            self.add(self.links.at(dz, 0), self.b, self.by_in[0, 1, dz + 3], self.by_in[1, 1, dz + 3])

    def ay(self, step):
        at = self.links.at
        if step > 1:
            self.wait("ay", 1)
            for way in WAYS:
                rows = self.a_half[way]
                self.add(at(0, way), rows, self.ay_in[(way + 1) // 2, 0, pl.ds(0, rows[1])])
        self.pair(
            ("ay", step),
            "y",
            lambda way: at(0, way * (3 - step)),
            self.a,
            self.a_half if step == 1 else None,
            lambda way, size: self.ay_in.at[(way + 1) // 2, step - 1, pl.ds(0, size)],
        )

    def bz(self, step):
        at = self.links.at
        if step > 1:
            self.wait("bz", step - 1)
            for way in WAYS:
                rows = self.b if step > 2 else self.b_half[way]
                got = self.bz_in[(way + 1) // 2, step - 2, pl.ds(0, rows[1])]
                self.add(at(way * (5 - step), 0), rows, got)
        self.pair(
            ("bz", step),
            "z",
            lambda way: at(way * (5 - step), 0),
            self.b,
            self.b_half if step == 1 else None,
            lambda way, size: self.bz_in.at[(way + 1) // 2, step - 1, pl.ds(0, size)],
        )

    def begin(self):
        self.az(1, 2)
        self.by(1, 4)
        self.az(1, 1, -1)
        self.by(1, -3, 3)
        self.az(1, 0)
        self.by(1, -2, 2)

    def steps(self):
        return [
            lambda: self.az(2, 2),
            lambda: self.by(2, 4),
            lambda: self.az(2, 1, -1),
            lambda: (self.by(2, -3, 3), self.by(1, -1, 1)),
            lambda: self.az(2, 0),
            lambda: self.az(3, 2),
            lambda: (self.by_done(4), self.bz(1)),
            lambda: (self.by(2, -2, 2), self.by(1, 0)),
            lambda: self.az(3, 1, -1),
            lambda: (self.by_done(-3, 3), self.bz(2)),
            lambda: self.az(3, 0),
            lambda: self.az(4, 2),
            lambda: self.by(2, -1, 1),
            lambda: (self.by_done(-2, 2), self.bz(3)),
            lambda: self.az(4, 1, -1),
            lambda: self.by(2, 0),
            lambda: (self.az_done(2), self.ay(1)),
            lambda: (self.by_done(-1, 1), self.bz(4)),
            lambda: self.az(4, 0),
            lambda: (self.az_done(1, -1), self.ay(2)),
            lambda: self.by_done(0),
            lambda: self.az_done(0),
        ]

    def upper(self):
        self.wait("ay", 2)
        total = self.ref[self.links.place, pl.ds(*self.a)].astype(F32)
        return total + self.ay_in[0, 1].astype(F32) + self.ay_in[1, 1].astype(F32)

    def lower(self):
        self.wait("bz", 4)
        total = self.ref[self.links.place, pl.ds(*self.b)].astype(F32)
        return total + self.bz_in[0, 3].astype(F32) + self.bz_in[1, 3].astype(F32)


def blended(steps, more, start=0.0, end=1.0):
    out, done = [], 0
    for i, step in enumerate(steps):
        reached = (i / len(steps) - start) / (end - start)
        upto = min(len(more), max(0, int(len(more) * reached)))
        out += more[done:upto]
        done = max(done, upto)
        out.append(step)
    return out + more[done:]


def kernel(
    out_ids, val_ids, out_count, val_count, gain, x_hbm, u_hbm, q_hbm, k_hbm, out_hbm, val_hbm,
    grad_input, out_grad, value_grad,
    gu, gx, xin, qin, kin, t_out, t_val, place_out, pick_out, place_val, pick_val, dense, w_out, w_val, probs, part,
    acc, wide_grads, vals, grads, scaled, att_t, az_in, by_in, ay_in, bz_in, final, passed,
    load_sems, send_sems, recv_sems,
):
    links = Links(recv_sems)
    place = links.place
    section = lax.axis_index("section")
    sections = lax.axis_size("section")
    before, after = (section + sections - 1) % sections, (section + 1) % sections

    loads = [
        pltpu.make_async_copy(src, dst, load_sems.at[i])
        for i, (src, dst) in enumerate(
            (
                (u_hbm.at[0], gu.at[place]),
                (x_hbm.at[0], xin),
                (out_hbm.at[0], t_out),
                (val_hbm.at[0], t_val),
                (q_hbm.at[0], qin),
                (k_hbm.at[0], kin),
            )
        )
    ]
    for load in loads:
        load.start()

    barrier = pltpu.get_barrier_semaphore()
    for to in links.to.values():
        pl.semaphore_signal(
            barrier, inc=1, device_id={"tensor": to}, device_id_type=pl.DeviceIdType.MESH
        )
    for to in (before, after):
        pl.semaphore_signal(
            barrier, inc=1, device_id={"section": to}, device_id_type=pl.DeviceIdType.MESH
        )

    gather_u = Gather(links, gu, TOK, CUT_U, send_sems.at[0])
    gather_x = Gather(links, gx, TOK + EXTRA, CUT_X, send_sems.at[1])
    scatter = Scatter(links, part, CUT_P, send_sems.at[2], az_in, by_in, ay_in, bz_in)

    lane = lax.broadcasted_iota(jnp.int32, (HALF, HEAD), 1)
    left = lane < EDGE
    rows_at = lax.broadcasted_iota(jnp.int32, (WIDTH, WIDTH), 0)
    cols_at = lax.broadcasted_iota(jnp.int32, (WIDTH, WIDTH), 1)
    inner = cols_at % EDGE
    natural = cols_at - inner + 2 * (inner % HALF) + inner // HALF
    order = (rows_at == natural).astype(F32).astype(BF)
    same = rows_at == cols_at

    def pair_out(first, second):
        evens = jnp.where(left, first, pltpu.roll(second, EDGE, 1))
        odds = jnp.where(left, pltpu.roll(first, EDGE, 1), second)
        return evens, odds

    def prepare_x():
        loads[1].wait()
        x = xin[...].astype(F32)
        row = pl.multiple_of(place * WIDTH, WIDTH)
        scaled_x = (x * gain[0:1, pl.ds(row, WIDTH)].astype(F32)).astype(BF)
        gx[place, pl.ds(0, TOK)] = dot(scaled_x, order).astype(BF)
        squares = jnp.sum(x * x, axis=1, keepdims=True)
        flat = jnp.sum(jnp.where(same, squares, 0.0), axis=0, keepdims=True)
        high = flat.astype(BF).astype(F32)
        middle = (flat - high).astype(BF).astype(F32)
        low = flat - high - middle
        at_row = lax.broadcasted_iota(jnp.int32, (EXTRA, TOK), 0)
        ride = jnp.where(at_row == 0, high, jnp.where(at_row == 1, middle, jnp.where(at_row == 2, low, 0.0)))
        gx[place, pl.ds(TOK, EXTRA)] = ride.astype(BF)

    def placers(ids, count, placer, picker):
        position = lax.broadcasted_iota(jnp.int32, (TILES, CAP), 0)
        slot = lax.broadcasted_iota(jnp.int32, (TILES, CAP), 1)
        held = (position == ids[...]) & (slot < count[...])
        placer[...] = held.astype(F32).astype(BF)
        across = lax.broadcasted_iota(jnp.int32, (CAP, CAP), 0) == lax.broadcasted_iota(jnp.int32, (CAP, CAP), 1)
        picker[...] = dot(across.astype(F32).astype(BF), placer[...], NT).astype(BF)

    def spread(tiles, placer, first, last):
        @pl.loop(first, last)
        def _(k):
            cols = pl.ds(pl.multiple_of(k * 256, 256), 256)
            for upper in range(0, TILES, 256):
                placed = dot(placer[pl.ds(upper, 256), :], tiles[:, cols])
                for row in range(0, 256, 8):
                    for side in range(2):
                        at = (upper + row) * 32 + 2 * k + side
                        dense[pl.ds(at, 8, stride=32), :] = placed[row : row + 8, side * HEAD : (side + 1) * HEAD]

    def gather_back(tiles, picker, first, last):
        @pl.loop(first, last)
        def _(k):
            cols = pl.ds(pl.multiple_of(k * 256, 256), 256)
            sides = [
                jnp.concatenate(
                    [dense[pl.ds(row * 32 + 2 * k + side, 8, stride=32), :] for row in range(0, TILES, 8)], axis=0
                ).astype(BF)
                for side in range(2)
            ]
            tiles[:, cols] = dot(picker[...], jnp.concatenate(sides, axis=1)).astype(BF)

    def tile(at):
        return dense[pl.ds(pl.multiple_of(at * 32, 32), 32), :]

    def build_out(first, last):
        @pl.loop(first, last)
        def _(g):
            for r in range(4):
                for pair in range(2):
                    at = r * COLS + g * 4 + 2 * pair
                    evens, odds = pair_out(tile(at), tile(at + 1))
                    cols = pl.ds(pair * HEAD, HEAD)
                    w_out[g, pl.ds(r * EDGE, HALF), cols] = evens.astype(BF)
                    w_out[g, pl.ds(r * EDGE + HALF, HALF), cols] = odds.astype(BF)

    def build_val(first, last):
        @pl.loop(first, last)
        def _(g):
            for c in range(4):
                for pair in range(2):
                    at = 2 * pair * COLS + g * 4 + c
                    evens, odds = pair_out(tile(at), tile(at + COLS))
                    cols = pl.ds(pair * HEAD, HEAD)
                    w_val[g, pl.ds(c * EDGE, HALF), cols] = evens.astype(BF)
                    w_val[g, pl.ds(c * EDGE + HALF, HALF), cols] = odds.astype(BF)

    def attention(head):
        cols = pl.ds(head * HEAD, HEAD)
        scores = dot(qin[:, cols], kin[:, cols], NT) * HEAD ** (-0.5)
        scores = jnp.where(rows_at >= cols_at, scores, -1e30)
        weights = jnp.exp(scores - jnp.max(scores, axis=1, keepdims=True))
        probs[head] = (weights / jnp.sum(weights, axis=1, keepdims=True)).astype(BF)

    def mixed(first, last):
        total = None
        for g in range(first, last):
            term = dot(gu[g], w_out[g], NT)
            total = term if total is None else total + term
        acc[...] = total if first == 0 else acc[...] + total

    def value_grads():
        mixed_grad = dot(acc[...].astype(BF), order, NT).astype(BF)
        for head in range(2):
            cols = pl.ds(head * HEAD, HEAD)
            back = dot(probs[head], mixed_grad[:, head * HEAD : (head + 1) * HEAD], TN)
            wide_grads[:, cols] = back
            grads[:, cols] = back.astype(BF)

    def partial_terms(first, last):
        for g in range(first, last):
            part[g] = dot(grads[...], w_val[g], NT).astype(BF)

    def values(first, last):
        total = None
        for g in range(first, last):
            term = dot(gx[g, pl.ds(0, TOK)], w_val[g])
            total = term if total is None else total + term
        acc[...] = total if first == 0 else acc[...] + total

    def attended():
        ride = jnp.zeros((EXTRA, TOK), F32)
        for g in range(BLOCKS):
            ride = ride + gx[g, pl.ds(TOK, EXTRA)].astype(F32)
        flat = jnp.sum(ride, axis=0, keepdims=True)
        squares = jnp.sum(jnp.where(same, flat, 0.0), axis=1, keepdims=True)
        inverse = lax.rsqrt(squares / MODEL + EPS)
        vals[...] = (acc[...] * inverse).astype(BF)
        scaled[...] = (wide_grads[...] * inverse).astype(BF)
        for head in range(2):
            cols = pl.ds(head * HEAD, HEAD)
            grads[:, cols] = dot(probs[head], vals[:, cols]).astype(BF)
        att_t[...] = dot(order, grads[...], (((0,), (1,)), ((), ()))).astype(BF)

    def put(at, value):
        dense[pl.ds(pl.multiple_of(at * 32, 32), 32), :] = value

    def full_out(first, last):
        @pl.loop(first, last)
        def _(g):
            block = dot(att_t[...], gu[g])
            for r in range(4):
                for pair in range(2):
                    cols = slice(pair * HEAD, (pair + 1) * HEAD)
                    evens = block[r * EDGE : r * EDGE + HALF, cols]
                    odds = block[r * EDGE + HALF : (r + 1) * EDGE, cols]
                    one, two = pair_out(evens, odds)
                    at = r * COLS + g * 4 + 2 * pair
                    put(at, one)
                    put(at + 1, two)

    def full_val(first, last):
        @pl.loop(first, last)
        def _(g):
            block = dot(gx[g, pl.ds(0, TOK)], scaled[...], TN)
            for c in range(4):
                for pair in range(2):
                    cols = slice(pair * HEAD, (pair + 1) * HEAD)
                    evens = block[c * EDGE : c * EDGE + HALF, cols]
                    odds = block[c * EDGE + HALF : (c + 1) * EDGE, cols]
                    one, two = pair_out(evens, odds)
                    at = 2 * pair * COLS + g * 4 + c
                    put(at, one)
                    put(at + COLS, two)

    def cut(function, parts, total, *given):
        size = total // parts
        return [lambda i=i: function(*given, i * size, (i + 1) * size) for i in range(parts)]

    stores = [
        pltpu.make_async_copy(t_out, out_grad.at[0], load_sems.at[6]),
        pltpu.make_async_copy(t_val, value_grad.at[0], load_sems.at[7]),
    ]

    alone = [
        lambda: placers(out_ids, out_count, place_out, pick_out),
        lambda: placers(val_ids, val_count, place_val, pick_val),
        loads[2].wait,
        *cut(spread, 8, 16, t_out, place_out),
        *cut(build_out, 8, BLOCKS),
        loads[3].wait,
        *cut(spread, 8, 16, t_val, place_val),
        *cut(build_val, 8, BLOCKS),
        loads[4].wait,
        loads[5].wait,
        lambda: attention(0),
        lambda: attention(1),
    ]
    back = [*cut(mixed, 8, BLOCKS), value_grads, *cut(partial_terms, 8, BLOCKS), scatter.begin]
    beside = [
        *cut(values, 8, BLOCKS),
        attended,
        *cut(full_out, 8, BLOCKS),
        *cut(gather_back, 8, 16, t_out, pick_out),
        stores[0].start,
        *cut(full_val, 8, BLOCKS),
        *cut(gather_back, 8, 16, t_val, pick_val),
        stores[1].start,
    ]

    loads[0].wait()
    pl.semaphore_wait(barrier, 6)
    gather_u.begin()
    prepare_x()

    steps_x = [gather_x.begin, *gather_x.steps()]
    early, middle = X_CUTS
    plan = blended(blended(gather_u.steps(), steps_x[:early], X_START), alone, 0.0, 1.0)
    plan += blended(back, steps_x[early:middle])
    sums = scatter.steps()
    plan += blended(sums[:SUMS_FIRST], steps_x[middle:])
    plan += blended(sums[SUMS_FIRST:], beside)
    for step in plan:
        step()

    def finish(rows, total):
        high = total.astype(BF)
        low = (total - high.astype(F32)).astype(BF)
        summed = dot(high, order, NT) + dot(low, order, NT)
        final[pl.ds(*rows)] = (gu[place, pl.ds(*rows)].astype(F32) + summed).astype(BF)

    finish(scatter.b, scatter.lower())
    finish(scatter.a, scatter.upper())

    hand_on = pltpu.make_async_remote_copy(
        src_ref=final,
        dst_ref=passed,
        send_sem=load_sems.at[9],
        recv_sem=load_sems.at[10],
        device_id={"section": before},
        device_id_type=pl.DeviceIdType.MESH,
    )

    @pl.when(section > 0)
    def _():
        hand_on.start()

    @pl.when(section == sections - 1)
    def _():
        passed[...] = jnp.zeros_like(passed)

    for routes in (gather_u, gather_x, scatter):
        routes.sent()

    @pl.when(section < sections - 1)
    def _():
        hand_on.wait_recv()

    last = pltpu.make_async_copy(passed, grad_input.at[0], load_sems.at[8])
    last.start()

    @pl.when(section > 0)
    def _():
        hand_on.wait_send()

    for store in stores:
        store.wait()
    last.wait()


X_CUTS = (9, 16)
X_START = 0.25
SUMS_FIRST = 6
PAIRS = 3 * 38


def backward(x, u, q, k, gain, out_tiles, out_ids, out_count, val_tiles, val_ids, val_count):
    vmem = pl.BlockSpec(memory_space=pltpu.VMEM)
    hbm = pl.BlockSpec(memory_space=pl.ANY)
    rest = TOK - CUT_P
    return pl.pallas_call(
        kernel,
        out_shape=(
            jax.ShapeDtypeStruct((1, TOK, WIDTH), BF),
            jax.ShapeDtypeStruct((1, CAP, EDGE * EDGE), BF),
            jax.ShapeDtypeStruct((1, CAP, EDGE * EDGE), BF),
        ),
        in_specs=[vmem] * 5 + [hbm] * 6,
        out_specs=(hbm, hbm, hbm),
        scratch_shapes=[
            pltpu.VMEM((BLOCKS, TOK, WIDTH), BF),
            pltpu.VMEM((BLOCKS, TOK + EXTRA, WIDTH), BF),
            pltpu.VMEM((TOK, WIDTH), BF),
            pltpu.VMEM((TOK, WIDTH), BF),
            pltpu.VMEM((TOK, WIDTH), BF),
            pltpu.VMEM((CAP, EDGE * EDGE), BF),
            pltpu.VMEM((CAP, EDGE * EDGE), BF),
            pltpu.VMEM((TILES, CAP), BF),
            pltpu.VMEM((CAP, TILES), BF),
            pltpu.VMEM((TILES, CAP), BF),
            pltpu.VMEM((CAP, TILES), BF),
            pltpu.VMEM((TILES * 32, HEAD), F32),
            pltpu.VMEM((BLOCKS, WIDTH, WIDTH), BF),
            pltpu.VMEM((BLOCKS, WIDTH, WIDTH), BF),
            pltpu.VMEM((2, TOK, TOK), BF),
            pltpu.VMEM((BLOCKS, TOK, WIDTH), BF),
            pltpu.VMEM((TOK, WIDTH), F32),
            pltpu.VMEM((TOK, WIDTH), F32),
            pltpu.VMEM((TOK, WIDTH), BF),
            pltpu.VMEM((TOK, WIDTH), BF),
            pltpu.VMEM((TOK, WIDTH), BF),
            pltpu.VMEM((WIDTH, TOK), BF),
            pltpu.VMEM((2, 4, NY, CUT_P, WIDTH), BF),
            pltpu.VMEM((2, 2, NZ, rest, WIDTH), BF),
            pltpu.VMEM((2, 2, CUT_P, WIDTH), BF),
            pltpu.VMEM((2, 4, rest, WIDTH), BF),
            pltpu.VMEM((TOK, WIDTH), BF),
            pltpu.VMEM((TOK, WIDTH), BF),
            pltpu.SemaphoreType.DMA((11,)),
            pltpu.SemaphoreType.DMA((3,)),
            pltpu.SemaphoreType.DMA((PAIRS,)),
        ],
        compiler_params=pltpu.CompilerParams(
            collective_id=0, has_side_effects=True, vmem_limit_bytes=46 * 1024 * 1024
        ),
        cost_estimate=pl.CostEstimate(flops=12 * 2**30, bytes_accessed=12 * 2**20, transcendentals=2**17),
    )(out_ids, val_ids, out_count, val_count, gain, x, u, q, k, out_tiles, val_tiles)


def per_device(
    layer_input, upstream, query_rows, key_rows, norm_gain, out_tiles, out_ids, out_count, value_tiles, value_ids,
    value_count,
):
    return backward(
        layer_input,
        upstream,
        query_rows,
        key_rows,
        norm_gain,
        out_tiles,
        out_ids,
        out_count,
        value_tiles,
        value_ids,
        value_count,
    )


def solution(mesh):
    rows = P("section", None, "tensor")
    tiles = P("section", "tensor", None)
    pair = P("section", "tensor")
    return jax.shard_map(
        per_device,
        mesh=mesh,
        in_specs=(rows, rows, rows, rows, P("section", None), tiles, pair, pair, tiles, pair, pair),
        out_specs=(rows, tiles, tiles),
        check_vma=False,
    )
```

time: 606 us -> 134 us (0.22)
  waiting for transfers between devices: 219 us -> 0 us
  matrix products: 179 us -> 0 us
  Pallas kernels: 0 us -> 122 us
  local copies, waits for them, and re-layouts: 97.2 us -> 9.37 us
  blocking collectives: 64.6 us -> 0 us
  other arithmetic: 19.1 us -> 0 us
  between operations: 15.2 us -> 1.95 us
  starting transfers between devices: 7.91 us -> 0 us
    dot_general x64 -> x0, matrix products: 179 us -> none  [the longest x30 84 us: select_blocks(): jnp.einsum('tck,gc->tgk', blocked, selector, preferred_element_type=jnp.f...]
    pallas_call x0 -> x1, Pallas kernels: none -> 122 us  [backward(): pl.pallas_call(kernel, out_shape=(jax.ShapeDtypeStruct((1, TOK, WIDTH), B...]
    all_gather x2 -> x0, waiting for transfers between devices: 115 us -> none  [the longest x1 75.4 us: per_device(): lax.all_gather(grads_here, 'tensor', axis=1, tiled=True)]
    reduce_scatter x1 -> x0, waiting for transfers between devices: 104 us -> none  [per_device(): lax.psum_scatter(partial_terms.astype(jnp.bfloat16), 'tensor', scatter_di...]
    psum x1 -> x0, blocking collectives: 64.6 us -> none  [per_device(): squares = lax.psum(jnp.sum(wide * wide, axis=-1, keepdims=True), 'tensor')]
    reshape x22 -> x0, local copies, waits for them, and re-layouts: 38.4 us -> none  [the longest x1 12.1 us: per_device(): value_grid.transpose(1, 2, 0, 3).reshape(model_width, local_width)]
    while x6 -> x0, local copies, waits for them, and re-layouts: 14 us -> none  [the longest x4 13.8 us: sparse_product(): lax.fori_loop(0, (filled + group_len - 1) // group_len, sparse_one_group,...]
    lt x21 -> x0, other arithmetic: 13.1 us -> none  [the longest x10 6.54 us: tile_one_group(): present = start_slot + jnp.arange(group_len, dtype=jnp.int32) < filled]
  transfers between devices with their start and end apart: 4 -> 0, of which waited for: 3 -> 0; matrix products, arithmetic and copies ran while one was open for 36% -> 0% of each run, Pallas kernels for 0% -> 0%
where the time goes in v1:
time: 134 us; the launch traced here: 133 us
  Pallas kernels  122 us (91%)
  local copies, waits for them, and re-layouts  9.37 us (7%)
  between operations  1.95 us (1%)
    pallas_call x1, Pallas kernels, backward(): pl.pallas_call(kernel, out_shape=(jax.ShapeDtypeStruct((1, TOK, WIDTH), B...  122 us
    unnamed x17, local copies, waits for them, and re-layouts  9.37 us

profile of v1, /device:TPU:1, one launch (start us, length us, event | category | flops | bytes accessed | tf_op | source)
XLA Modules:
  0.0 132.9 jit_solution(13352124246697612813)
XLA Ops:
  1.9 0.0 copy-start
  1.9 0.9 copy-done
  2.8 0.0 copy-start.1
  2.8 0.9 copy-done.1
  3.7 0.0 copy-start.2
  3.7 0.9 copy-done.2
  4.6 0.0 copy-start.3
  4.6 0.9 copy-done.3
  5.5 0.0 copy-start.4
  5.5 0.8 copy-done.4
  6.3 0.0 copy-start.5
  6.3 0.7 copy-done.5
  7.0 0.0 copy-start.6
  7.0 0.7 copy-done.6
  7.7 121.6 %shard_map.130 = (bf16[1,256,256]{2,1,0:T(8,128)(2,1)S(1)}, bf16[1,320,4096]{2,1,0:T(8,128)(2,1)S(1)}, bf16[1,320,4096]{2,1,0:T(8,128)(2,1)S(1)}) custom-call(s32[1,320]{1,0:T(1,128)S(1)} %copy-done.5, s32[1,320]{1,0:T(1,128)S(1)} %copy-done.6, s32[1,1]{1,0:T(1,128)S(6)} %copy.17.out_count, s32[1,1]{1,0:T(1,128)S(6)} %copy.18.val_count, ...), custom_call_target="tpu_custom_call" | custom-call | flops 12884901888 | bytes 12582912 | tf_op jit(solution)/shard_map/pallas_call | solution.py:652
  129.3 0.7 copy.19
  129.9 1.5 %copy.20 = bf16[1,320,4096]{2,1,0:T(8,128)(2,1)} copy(bf16[1,320,4096]{2,1,0:T(8,128)(2,1)S(1)} %get-tuple-element.7) | data formatting | bytes 5242880
  131.4 1.5 %copy.21 = bf16[1,320,4096]{2,1,0:T(8,128)(2,1)} copy(bf16[1,320,4096]{2,1,0:T(8,128)(2,1)S(1)} %get-tuple-element.8) | data formatting | bytes 5242880
Async XLA Ops:
  1.9 0.9 copy-start
  2.8 0.9 copy-start.1
  3.7 0.9 copy-start.2
  4.6 0.9 copy-start.3
  5.5 0.8 copy-start.4
  6.3 0.7 copy-start.5
  7.0 0.7 copy-start.6

commit v2 on v1

--- a/solution.py
+++ b/solution.py
@@ -20,6 +20,7 @@
 CUT_U, CUT_X, CUT_P = 96, 112, 112
 EXTRA = 16
 BLOCKS = NZ * NY
+PITCH = 33
 
 BF = jnp.bfloat16
 F32 = jnp.float32
@@ -339,13 +340,14 @@
 
 
 def kernel(
-    out_ids, val_ids, out_count, val_count, gain, x_hbm, u_hbm, q_hbm, k_hbm, out_hbm, val_hbm,
+    out_ids_hbm, val_ids_hbm, out_count_hbm, val_count_hbm, gain_hbm, x_hbm, u_hbm, q_hbm, k_hbm, out_hbm, val_hbm,
     grad_input, out_grad, value_grad,
-    gu, gx, xin, qin, kin, t_out, t_val, place_out, pick_out, place_val, pick_val, dense, w_out, w_val, probs, part,
+    out_ids, val_ids, out_count, val_count, gain, gu, gx, xin, qin, kin, t_out, t_val, place_out, pick_out, place_val, pick_val, dense, w_out, w_val, probs, probs_t,
     acc, wide_grads, vals, grads, scaled, att_t, az_in, by_in, ay_in, bz_in, final, passed,
     load_sems, send_sems, recv_sems,
 ):
     links = Links(recv_sems)
+    part = w_out
     place = links.place
     section = lax.axis_index("section")
     sections = lax.axis_size("section")
@@ -361,6 +363,11 @@
                 (val_hbm.at[0], t_val),
                 (q_hbm.at[0], qin),
                 (k_hbm.at[0], kin),
+                (gain_hbm, gain),
+                (out_ids_hbm, out_ids),
+                (val_ids_hbm, val_ids),
+                (out_count_hbm, out_count),
+                (val_count_hbm, val_count),
             )
         )
     ]
@@ -397,6 +404,7 @@
 
     def prepare_x():
         loads[1].wait()
+        loads[6].wait()
         x = xin[...].astype(F32)
         row = pl.multiple_of(place * WIDTH, WIDTH)
         scaled_x = (x * gain[0:1, pl.ds(row, WIDTH)].astype(F32)).astype(BF)
@@ -419,33 +427,33 @@
         picker[...] = dot(across.astype(F32).astype(BF), placer[...], NT).astype(BF)
 
     def spread(tiles, placer, first, last):
-        @pl.loop(first, last)
+        @pl.loop(first, last, unroll=2)
         def _(k):
             cols = pl.ds(pl.multiple_of(k * 256, 256), 256)
             for upper in range(0, TILES, 256):
                 placed = dot(placer[pl.ds(upper, 256), :], tiles[:, cols])
                 for row in range(0, 256, 8):
                     for side in range(2):
-                        at = (upper + row) * 32 + 2 * k + side
-                        dense[pl.ds(at, 8, stride=32), :] = placed[row : row + 8, side * HEAD : (side + 1) * HEAD]
+                        at = (upper + row) * PITCH + 2 * k + side
+                        dense[pl.ds(at, 8, stride=PITCH), :] = placed[row : row + 8, side * HEAD : (side + 1) * HEAD]
 
     def gather_back(tiles, picker, first, last):
-        @pl.loop(first, last)
+        @pl.loop(first, last, unroll=2)
         def _(k):
             cols = pl.ds(pl.multiple_of(k * 256, 256), 256)
             sides = [
                 jnp.concatenate(
-                    [dense[pl.ds(row * 32 + 2 * k + side, 8, stride=32), :] for row in range(0, TILES, 8)], axis=0
+                    [dense[pl.ds(row * PITCH + 2 * k + side, 8, stride=PITCH), :] for row in range(0, TILES, 8)], axis=0
                 ).astype(BF)
                 for side in range(2)
             ]
             tiles[:, cols] = dot(picker[...], jnp.concatenate(sides, axis=1)).astype(BF)
 
     def tile(at):
-        return dense[pl.ds(pl.multiple_of(at * 32, 32), 32), :]
+        return dense[pl.ds(at * PITCH, 32), :]
 
     def build_out(first, last):
-        @pl.loop(first, last)
+        @pl.loop(first, last, unroll=4)
         def _(g):
             for r in range(4):
                 for pair in range(2):
@@ -456,7 +464,7 @@
                     w_out[g, pl.ds(r * EDGE + HALF, HALF), cols] = odds.astype(BF)
 
     def build_val(first, last):
-        @pl.loop(first, last)
+        @pl.loop(first, last, unroll=4)
         def _(g):
             for c in range(4):
                 for pair in range(2):
@@ -472,6 +480,7 @@
         scores = jnp.where(rows_at >= cols_at, scores, -1e30)
         weights = jnp.exp(scores - jnp.max(scores, axis=1, keepdims=True))
         probs[head] = (weights / jnp.sum(weights, axis=1, keepdims=True)).astype(BF)
+        probs_t[head] = probs[head].T
 
     def mixed(first, last):
         total = None
@@ -484,7 +493,7 @@
         mixed_grad = dot(acc[...].astype(BF), order, NT).astype(BF)
         for head in range(2):
             cols = pl.ds(head * HEAD, HEAD)
-            back = dot(probs[head], mixed_grad[:, head * HEAD : (head + 1) * HEAD], TN)
+            back = dot(probs_t[head], mixed_grad[:, head * HEAD : (head + 1) * HEAD])
             wide_grads[:, cols] = back
             grads[:, cols] = back.astype(BF)
 
@@ -514,10 +523,10 @@
         att_t[...] = dot(order, grads[...], (((0,), (1,)), ((), ()))).astype(BF)
 
     def put(at, value):
-        dense[pl.ds(pl.multiple_of(at * 32, 32), 32), :] = value
+        dense[pl.ds(at * PITCH, 32), :] = value
 
     def full_out(first, last):
-        @pl.loop(first, last)
+        @pl.loop(first, last, unroll=4)
         def _(g):
             block = dot(att_t[...], gu[g])
             for r in range(4):
@@ -531,7 +540,7 @@
                     put(at + 1, two)
 
     def full_val(first, last):
-        @pl.loop(first, last)
+        @pl.loop(first, last, unroll=4)
         def _(g):
             block = dot(gx[g, pl.ds(0, TOK)], scaled[...], TN)
             for c in range(4):
@@ -549,11 +558,12 @@
         return [lambda i=i: function(*given, i * size, (i + 1) * size) for i in range(parts)]
 
     stores = [
-        pltpu.make_async_copy(t_out, out_grad.at[0], load_sems.at[6]),
-        pltpu.make_async_copy(t_val, value_grad.at[0], load_sems.at[7]),
+        pltpu.make_async_copy(t_out, out_grad.at[0], load_sems.at[11]),
+        pltpu.make_async_copy(t_val, value_grad.at[0], load_sems.at[12]),
     ]
 
     alone = [
+        *(loads[i].wait for i in (7, 8, 9, 10)),
         lambda: placers(out_ids, out_count, place_out, pick_out),
         lambda: placers(val_ids, val_count, place_val, pick_val),
         loads[2].wait,
@@ -606,8 +616,8 @@
     hand_on = pltpu.make_async_remote_copy(
         src_ref=final,
         dst_ref=passed,
-        send_sem=load_sems.at[9],
-        recv_sem=load_sems.at[10],
+        send_sem=load_sems.at[14],
+        recv_sem=load_sems.at[15],
         device_id={"section": before},
         device_id_type=pl.DeviceIdType.MESH,
     )
@@ -627,7 +637,7 @@
     def _():
         hand_on.wait_recv()
 
-    last = pltpu.make_async_copy(passed, grad_input.at[0], load_sems.at[8])
+    last = pltpu.make_async_copy(passed, grad_input.at[0], load_sems.at[13])
     last.start()
 
     @pl.when(section > 0)
@@ -646,8 +656,8 @@
 
 
 def backward(x, u, q, k, gain, out_tiles, out_ids, out_count, val_tiles, val_ids, val_count):
-    vmem = pl.BlockSpec(memory_space=pltpu.VMEM)
-    hbm = pl.BlockSpec(memory_space=pl.ANY)
+    hbm = pl.BlockSpec(memory_space=pltpu.HBM)
+    some = pl.BlockSpec(memory_space=pl.ANY)
     rest = TOK - CUT_P
     return pl.pallas_call(
         kernel,
@@ -656,9 +666,14 @@
             jax.ShapeDtypeStruct((1, CAP, EDGE * EDGE), BF),
             jax.ShapeDtypeStruct((1, CAP, EDGE * EDGE), BF),
         ),
-        in_specs=[vmem] * 5 + [hbm] * 6,
-        out_specs=(hbm, hbm, hbm),
+        in_specs=[hbm] * 11,
+        out_specs=(some, some, some),
         scratch_shapes=[
+            pltpu.VMEM((1, CAP), jnp.int32),
+            pltpu.VMEM((1, CAP), jnp.int32),
+            pltpu.VMEM((1, 1), jnp.int32),
+            pltpu.VMEM((1, 1), jnp.int32),
+            pltpu.VMEM((1, MODEL), BF),
             pltpu.VMEM((BLOCKS, TOK, WIDTH), BF),
             pltpu.VMEM((BLOCKS, TOK + EXTRA, WIDTH), BF),
             pltpu.VMEM((TOK, WIDTH), BF),
@@ -670,11 +685,11 @@
             pltpu.VMEM((CAP, TILES), BF),
             pltpu.VMEM((TILES, CAP), BF),
             pltpu.VMEM((CAP, TILES), BF),
-            pltpu.VMEM((TILES * 32, HEAD), F32),
+            pltpu.VMEM((TILES * PITCH, HEAD), F32),
             pltpu.VMEM((BLOCKS, WIDTH, WIDTH), BF),
             pltpu.VMEM((BLOCKS, WIDTH, WIDTH), BF),
             pltpu.VMEM((2, TOK, TOK), BF),
-            pltpu.VMEM((BLOCKS, TOK, WIDTH), BF),
+            pltpu.VMEM((2, TOK, TOK), BF),
             pltpu.VMEM((TOK, WIDTH), F32),
             pltpu.VMEM((TOK, WIDTH), F32),
             pltpu.VMEM((TOK, WIDTH), BF),
@@ -687,12 +702,12 @@
             pltpu.VMEM((2, 4, rest, WIDTH), BF),
             pltpu.VMEM((TOK, WIDTH), BF),
             pltpu.VMEM((TOK, WIDTH), BF),
-            pltpu.SemaphoreType.DMA((11,)),
+            pltpu.SemaphoreType.DMA((16,)),
             pltpu.SemaphoreType.DMA((3,)),
             pltpu.SemaphoreType.DMA((PAIRS,)),
         ],
         compiler_params=pltpu.CompilerParams(
-            collective_id=0, has_side_effects=True, vmem_limit_bytes=46 * 1024 * 1024
+            collective_id=0, has_side_effects=True, vmem_limit_bytes=60 * 1024 * 1024
         ),
         cost_estimate=pl.CostEstimate(flops=12 * 2**30, bytes_accessed=12 * 2**20, transcendentals=2**17),
     )(out_ids, val_ids, out_count, val_count, gain, x, u, q, k, out_tiles, val_tiles)

time: 134 us -> 107 us (0.80)
  Pallas kernels: 122 us -> 98.5 us
  local copies, waits for them, and re-layouts: 9.37 us -> 6.74 us
    pallas_call x1, Pallas kernels: 122 us -> 98.5 us  [backward(): pl.pallas_call(kernel, out_shape=(jax.ShapeDtypeStruct((1, TOK, WIDTH), B...]
    unnamed x17 -> x5, local copies, waits for them, and re-layouts: 9.37 us -> 6.74 us
where the time goes in v2:
time: 107 us
  Pallas kernels  98.5 us (92%)
  local copies, waits for them, and re-layouts  6.74 us (6%)
  between operations  1.94 us (2%)
    pallas_call x1, Pallas kernels, backward(): pl.pallas_call(kernel, out_shape=(jax.ShapeDtypeStruct((1, TOK, WIDTH), B...  98.5 us
    unnamed x5, local copies, waits for them, and re-layouts  6.74 us

profile of v2, /device:TPU:1, one launch (start us, length us, event | category | flops | bytes accessed | tf_op | source)
XLA Modules:
  0.0 107.2 jit_solution(17346177711578205)
XLA Ops:
  1.9 98.5 %shard_map.130 = (bf16[1,256,256]{2,1,0:T(8,128)(2,1)}, bf16[1,320,4096]{2,1,0:T(8,128)(2,1)}, bf16[1,320,4096]{2,1,0:T(8,128)(2,1)}) custom-call(s32[1,320]{1,0:T(1,128)} %out_ids_hbm.1, s32[1,320]{1,0:T(1,128)} %val_ids_hbm.1, s32[1,1]{1,0:T(1,128)S(6)} %copy.17.out_count_hbm, s32[1,1]{1,0:T(1,128)S(6)} %copy.18.val_count_hbm, bf16[1,8192]{1,0:T(2,128)(2,1)} %gain_hbm.1, ...), custom_call_target="tpu_custom_call" | custom-call | flops 12884901888 | bytes 12582912 | tf_op jit(solution)/shard_map/pallas_call | solution.py:662
  100.4 1.6 %copy.19 = bf16[1,256,256]{2,1,0:T(8,128)(2,1)} copy(bf16[1,256,256]{2,1,0:T(8,128)(2,1)} %get-tuple-element.6) | data formatting | bytes 262144
  102.0 0.0 copy-start
  102.0 3.7 %copy.20 = bf16[1,320,4096]{2,1,0:T(8,128)(2,1)} copy(bf16[1,320,4096]{2,1,0:T(8,128)(2,1)} %get-tuple-element.7) | data formatting | bytes 5242880
  105.7 0.0 copy-done
  105.7 1.5 %copy.21 = bf16[1,320,4096]{2,1,0:T(8,128)(2,1)} copy(bf16[1,320,4096]{2,1,0:T(8,128)(2,1)S(1)} %copy-done) | data formatting | bytes 5242880
Async XLA Ops:
  102.0 3.7 %copy-start = (bf16[1,320,4096]{2,1,0:T(8,128)(2,1)S(1)}, bf16[1,320,4096]{2,1,0:T(8,128)(2,1)}, u32[]{:S(2)}) copy-start(bf16[1,320,4096]{2,1,0:T(8,128)(2,1)} %get-tuple-element.8) | copy-start | bytes 7864324

commit v3 on v2

--- a/solution.py
+++ b/solution.py
@@ -17,7 +17,7 @@
 COLS = 128
 MODEL = 8192
 HALF = EDGE // 2
-CUT_U, CUT_X, CUT_P = 96, 112, 112
+CUT_U, CUT_X, CUT_P = 112, 112, 96
 EXTRA = 16
 BLOCKS = NZ * NY
 PITCH = 33
@@ -45,6 +45,7 @@
             ("z", -1): self.at(-1, 0),
             ("y", 1): self.at(0, 1),
             ("y", -1): self.at(0, -1),
+            ("y", 2): self.at(0, 2),
         }
 
     def at(self, dz, dy):
@@ -97,6 +98,11 @@
             view = self.ref.at[pl.ds(0, 2), pl.ds(0, rows[1])]
         self.coming[key] = (view, semaphore)
 
+    def across(self, src, dst):
+        semaphore = self.links.semaphore()
+        self.links.send(src, dst, "y", 2, self.send_sem, semaphore)
+        self.coming[("ay", 2)] = (self.ref.at[0, pl.ds(*self.a)], semaphore)
+
     def wait(self, *key):
         wait_for(*self.coming.pop(key))
 
@@ -105,17 +111,11 @@
 
 
 class Gather(Routes):
-    def ay(self, step):
-        at = self.links.at
-        if step > 1:
-            self.wait("ay", 1)
-        self.pair(
-            ("ay", step),
-            "y",
-            lambda way: at(0, -way * (step - 1)),
-            self.a,
-            self.a_half if step == 2 else None,
-        )
+    def ay(self):
+        place = self.links.place
+        self.pair(("ay", 1), "y", lambda way: place, self.a, None)
+        part = self.ref.at[place, pl.ds(*self.a)]
+        self.across(part, part)
 
     def az(self, step, *offsets):
         at = self.links.at
@@ -124,6 +124,8 @@
                 self.wait("az", dy, step - 1)
             elif dy == 2:
                 self.wait("ay", 2)
+            elif dy in (1, -1) and ("ay", 1) in self.coming:
+                self.wait("ay", 1)
             self.pair(
                 ("az", dy, step),
                 "z",
@@ -157,36 +159,8 @@
             self.wait("by", dz, 1)
             self.pair(("by", dz, 2), "y", lambda way: at(dz, -way), self.b, self.b_half)
 
-    def begin(self):
-        self.ay(1)
-        self.bz(1)
-        self.az(1, 0)
-        self.by1(0)
-
-    def steps(self):
-        return [
-            lambda: (self.ay(2), self.az(1, 1, -1)),
-            lambda: (self.bz(2), self.by1(-1, 1)),
-            lambda: self.az(2, 0),
-            lambda: self.by2(0),
-            lambda: self.az(1, 2),
-            lambda: self.az(2, 1, -1),
-            lambda: (self.bz(3), self.by1(-2, 2)),
-            lambda: self.az(3, 0),
-            lambda: self.by2(-1, 1),
-            lambda: self.az(2, 2),
-            lambda: self.az(3, 1, -1),
-            lambda: (self.bz(4), self.by1(-3, 3)),
-            lambda: self.az(4, 0),
-            lambda: self.by2(-2, 2),
-            lambda: self.az(3, 2),
-            lambda: self.az(4, 1, -1),
-            lambda: self.by1(4),
-            lambda: self.by2(-3, 3),
-            lambda: self.az(4, 2),
-            lambda: self.by2(4),
-            lambda: self.finish(),
-        ]
+    def moves(self):
+        return {"ay": self.ay, "az": self.az, "bz": self.bz, "by1": self.by1, "by2": self.by2, "finish": self.finish}
 
     def finish(self):
         for key in sorted(self.coming):
@@ -250,21 +224,19 @@
             self.wait("by", dz, 2)
             self.add(self.links.at(dz, 0), self.b, self.by_in[0, 1, dz + 3], self.by_in[1, 1, dz + 3])
 
-    def ay(self, step):
+    def ay(self):
         at = self.links.at
-        if step > 1:
-            self.wait("ay", 1)
-            for way in WAYS:
-                rows = self.a_half[way]
-                self.add(at(0, way), rows, self.ay_in[(way + 1) // 2, 0, pl.ds(0, rows[1])])
         self.pair(
-            ("ay", step),
+            ("ay", 1),
             "y",
-            lambda way: at(0, way * (3 - step)),
+            lambda way: at(0, way),
             self.a,
-            self.a_half if step == 1 else None,
-            lambda way, size: self.ay_in.at[(way + 1) // 2, step - 1, pl.ds(0, size)],
+            None,
+            lambda way, size: self.ay_in.at[(way + 1) // 2, pl.ds(0, size)],
         )
+
+    def ay_across(self):
+        self.across(self.ref.at[self.links.at(0, 2), pl.ds(*self.a)], self.ay_in.at[2])
 
     def bz(self, step):
         at = self.links.at
@@ -283,60 +255,29 @@
             lambda way, size: self.bz_in.at[(way + 1) // 2, step - 1, pl.ds(0, size)],
         )
 
-    def begin(self):
-        self.az(1, 2)
-        self.by(1, 4)
-        self.az(1, 1, -1)
-        self.by(1, -3, 3)
-        self.az(1, 0)
-        self.by(1, -2, 2)
-
-    def steps(self):
-        return [
-            lambda: self.az(2, 2),
-            lambda: self.by(2, 4),
-            lambda: self.az(2, 1, -1),
-            lambda: (self.by(2, -3, 3), self.by(1, -1, 1)),
-            lambda: self.az(2, 0),
-            lambda: self.az(3, 2),
-            lambda: (self.by_done(4), self.bz(1)),
-            lambda: (self.by(2, -2, 2), self.by(1, 0)),
-            lambda: self.az(3, 1, -1),
-            lambda: (self.by_done(-3, 3), self.bz(2)),
-            lambda: self.az(3, 0),
-            lambda: self.az(4, 2),
-            lambda: self.by(2, -1, 1),
-            lambda: (self.by_done(-2, 2), self.bz(3)),
-            lambda: self.az(4, 1, -1),
-            lambda: self.by(2, 0),
-            lambda: (self.az_done(2), self.ay(1)),
-            lambda: (self.by_done(-1, 1), self.bz(4)),
-            lambda: self.az(4, 0),
-            lambda: (self.az_done(1, -1), self.ay(2)),
-            lambda: self.by_done(0),
-            lambda: self.az_done(0),
-        ]
+    def moves(self):
+        return {
+            "az": self.az,
+            "az_done": self.az_done,
+            "by": self.by,
+            "by_done": self.by_done,
+            "bz": self.bz,
+            "ay": self.ay,
+            "ay_across": self.ay_across,
+        }
 
     def upper(self):
+        self.wait("ay", 1)
         self.wait("ay", 2)
         total = self.ref[self.links.place, pl.ds(*self.a)].astype(F32)
-        return total + self.ay_in[0, 1].astype(F32) + self.ay_in[1, 1].astype(F32)
+        for way in range(3):
+            total = total + self.ay_in[way].astype(F32)
+        return total
 
     def lower(self):
         self.wait("bz", 4)
         total = self.ref[self.links.place, pl.ds(*self.b)].astype(F32)
         return total + self.bz_in[0, 3].astype(F32) + self.bz_in[1, 3].astype(F32)
-
-
-def blended(steps, more, start=0.0, end=1.0):
-    out, done = [], 0
-    for i, step in enumerate(steps):
-        reached = (i / len(steps) - start) / (end - start)
-        upto = min(len(more), max(0, int(len(more) * reached)))
-        out += more[done:upto]
-        done = max(done, upto)
-        out.append(step)
-    return out + more[done:]
 
 
 def kernel(
@@ -563,46 +504,47 @@
     ]
 
     alone = [
-        *(loads[i].wait for i in (7, 8, 9, 10)),
-        lambda: placers(out_ids, out_count, place_out, pick_out),
+        lambda: ([loads[i].wait() for i in (7, 8, 9, 10)], placers(out_ids, out_count, place_out, pick_out)),
         lambda: placers(val_ids, val_count, place_val, pick_val),
-        loads[2].wait,
-        *cut(spread, 8, 16, t_out, place_out),
+        lambda: (loads[2].wait(), spread(t_out, place_out, 0, 2)),
+        *cut(spread, 8, 16, t_out, place_out)[1:],
         *cut(build_out, 8, BLOCKS),
-        loads[3].wait,
-        *cut(spread, 8, 16, t_val, place_val),
+        lambda: (loads[3].wait(), spread(t_val, place_val, 0, 2)),
+        *cut(spread, 8, 16, t_val, place_val)[1:],
         *cut(build_val, 8, BLOCKS),
-        loads[4].wait,
-        loads[5].wait,
-        lambda: attention(0),
+        lambda: (loads[4].wait(), loads[5].wait(), attention(0)),
         lambda: attention(1),
     ]
-    back = [*cut(mixed, 8, BLOCKS), value_grads, *cut(partial_terms, 8, BLOCKS), scatter.begin]
+    back = [*cut(mixed, 8, BLOCKS), value_grads, *cut(partial_terms, 8, BLOCKS)]
     beside = [
         *cut(values, 8, BLOCKS),
         attended,
         *cut(full_out, 8, BLOCKS),
-        *cut(gather_back, 8, 16, t_out, pick_out),
-        stores[0].start,
+        *cut(gather_back, 8, 16, t_out, pick_out)[:-1],
+        lambda: (gather_back(t_out, pick_out, 14, 16), stores[0].start()),
         *cut(full_val, 8, BLOCKS),
-        *cut(gather_back, 8, 16, t_val, pick_val),
-        stores[1].start,
+        *cut(gather_back, 8, 16, t_val, pick_val)[:-1],
+        lambda: (gather_back(t_val, pick_val, 14, 16), stores[1].start()),
     ]
 
     loads[0].wait()
-    pl.semaphore_wait(barrier, 6)
-    gather_u.begin()
-    prepare_x()
-
-    steps_x = [gather_x.begin, *gather_x.steps()]
-    early, middle = X_CUTS
-    plan = blended(blended(gather_u.steps(), steps_x[:early], X_START), alone, 0.0, 1.0)
-    plan += blended(back, steps_x[early:middle])
-    sums = scatter.steps()
-    plan += blended(sums[:SUMS_FIRST], steps_x[middle:])
-    plan += blended(sums[SUMS_FIRST:], beside)
-    for step in plan:
-        step()
+    pl.semaphore_wait(barrier, 7)
+
+    compute = {"alone": iter(alone), "back": iter(back), "beside": iter(beside)}
+    routes_of = {"u": gather_u, "x": gather_x, "p": scatter}
+    prepared = False
+    for where, what, *given in PLAN:
+        if where == "c":
+            next(compute[what])()
+            continue
+        if where == "x" and not prepared:
+            prepare_x()
+            prepared = True
+        moves = routes_of[where].moves()
+        moves[what](*given)
+    for rest in compute.values():
+        for step in rest:
+            step()
 
     def finish(rows, total):
         high = total.astype(BF)
@@ -610,21 +552,19 @@
         summed = dot(high, order, NT) + dot(low, order, NT)
         final[pl.ds(*rows)] = (gu[place, pl.ds(*rows)].astype(F32) + summed).astype(BF)
 
-    finish(scatter.b, scatter.lower())
-    finish(scatter.a, scatter.upper())
-
-    hand_on = pltpu.make_async_remote_copy(
-        src_ref=final,
-        dst_ref=passed,
-        send_sem=load_sems.at[14],
-        recv_sem=load_sems.at[15],
-        device_id={"section": before},
-        device_id_type=pl.DeviceIdType.MESH,
-    )
-
-    @pl.when(section > 0)
-    def _():
-        hand_on.start()
+    halves = []
+    for i, (rows, total) in enumerate(((scatter.b, scatter.lower), (scatter.a, scatter.upper))):
+        finish(rows, total())
+        hand_on = pltpu.make_async_remote_copy(
+            src_ref=final.at[pl.ds(*rows)],
+            dst_ref=passed.at[pl.ds(*rows)],
+            send_sem=load_sems.at[14 + i],
+            recv_sem=load_sems.at[16 + i],
+            device_id={"section": before},
+            device_id_type=pl.DeviceIdType.MESH,
+        )
+        halves.append(hand_on)
+        pl.when(section > 0)(hand_on.start)
 
     @pl.when(section == sections - 1)
     def _():
@@ -633,25 +573,58 @@
     for routes in (gather_u, gather_x, scatter):
         routes.sent()
 
-    @pl.when(section < sections - 1)
-    def _():
-        hand_on.wait_recv()
+    for hand_on in halves:
+        pl.when(section < sections - 1)(hand_on.wait_recv)
 
     last = pltpu.make_async_copy(passed, grad_input.at[0], load_sems.at[13])
     last.start()
 
-    @pl.when(section > 0)
-    def _():
-        hand_on.wait_send()
+    for hand_on in halves:
+        pl.when(section > 0)(hand_on.wait_send)
 
     for store in stores:
         store.wait()
     last.wait()
 
 
-X_CUTS = (9, 16)
-X_START = 0.25
-SUMS_FIRST = 6
+PLAN = (
+    ("u", "ay"), ("u", "bz", 1), ("u", "az", 1, 0), ("u", "by1", 0), ("c", "alone"), ("c", "alone"), ("c", "alone"),
+    ("c", "alone"), ("c", "alone"), ("x", "bz", 1), ("c", "alone"), ("c", "alone"), ("c", "alone"), ("c", "alone"),
+    ("x", "ay"), ("c", "alone"), ("c", "alone"), ("u", "az", 1, 1), ("u", "az", 1, -1), ("c", "alone"),
+    ("c", "alone"), ("u", "bz", 2), ("u", "by1", 1), ("u", "by1", -1), ("c", "alone"), ("c", "alone"),
+    ("c", "alone"), ("c", "alone"), ("u", "az", 1, 2), ("c", "alone"), ("c", "alone"), ("u", "az", 2, 0),
+    ("c", "alone"), ("c", "alone"), ("c", "alone"), ("c", "alone"), ("u", "by2", 0), ("c", "alone"), ("c", "alone"),
+    ("c", "alone"), ("c", "alone"), ("c", "alone"), ("c", "alone"), ("c", "alone"), ("c", "alone"), ("c", "alone"),
+    ("u", "az", 2, 1), ("c", "alone"), ("c", "alone"), ("c", "alone"), ("c", "alone"), ("u", "az", 2, -1),
+    ("x", "by1", 0), ("u", "by2", 1), ("u", "bz", 3), ("u", "by1", -2), ("u", "by1", 2), ("u", "by2", -1),
+    ("u", "az", 2, 2), ("u", "az", 3, 0), ("u", "az", 3, 1), ("u", "az", 3, -1), ("x", "by2", 0), ("u", "by2", -2),
+    ("u", "bz", 4), ("u", "by1", 3), ("u", "by1", -3), ("u", "by2", 2), ("u", "az", 3, 2), ("u", "az", 4, 0),
+    ("u", "az", 4, 1), ("u", "az", 4, -1), ("u", "by2", 3), ("x", "bz", 2), ("x", "by1", -1), ("u", "by1", 4),
+    ("u", "by2", -3), ("u", "az", 4, 2), ("x", "az", 1, 1), ("x", "by1", 1), ("x", "az", 1, -1), ("x", "az", 1, 0),
+    ("x", "by2", -1), ("u", "by2", 4), ("x", "bz", 3), ("x", "by1", 2), ("x", "az", 2, 1), ("x", "by2", 1),
+    ("x", "az", 2, -1), ("x", "by1", -2), ("u", "finish"), ("c", "back"), ("x", "az", 1, 2), ("c", "back"),
+    ("c", "back"), ("x", "bz", 4), ("c", "back"), ("x", "by1", 3), ("c", "back"), ("x", "az", 3, 1), ("c", "back"),
+    ("c", "back"), ("x", "by2", 2), ("c", "back"), ("x", "az", 2, 0), ("c", "back"), ("x", "by2", -2), ("c", "back"),
+    ("x", "az", 2, 2), ("c", "back"), ("x", "by1", -3), ("c", "back"), ("c", "back"), ("c", "back"), ("c", "back"),
+    ("c", "back"), ("x", "az", 3, -1), ("c", "back"), ("x", "by1", 4), ("x", "az", 4, 1), ("p", "az", 1, -1),
+    ("x", "by2", 3), ("x", "az", 3, 0), ("p", "by", 1, 4), ("x", "az", 3, 2), ("x", "by2", -3), ("x", "az", 4, -1),
+    ("p", "by", 1, -3), ("p", "az", 1, 1), ("x", "by2", 4), ("p", "az", 1, 0), ("p", "az", 1, 2), ("p", "by", 1, 3),
+    ("x", "az", 4, 0), ("p", "by", 2, 4), ("p", "az", 2, -1), ("x", "az", 4, 2), ("p", "az", 2, 1),
+    ("p", "by", 2, -3), ("p", "az", 2, 2), ("p", "by", 1, 2), ("p", "az", 2, 0), ("p", "by", 2, 3), ("x", "finish"),
+    ("p", "by_done", 4), ("p", "az", 3, -1), ("c", "beside"), ("c", "beside"), ("c", "beside"), ("p", "bz", 1),
+    ("p", "by", 1, -2), ("c", "beside"), ("p", "by_done", -3), ("p", "az", 3, 1), ("p", "by", 1, 1), ("c", "beside"),
+    ("c", "beside"), ("c", "beside"), ("p", "az", 3, 2), ("p", "by", 2, 2), ("c", "beside"), ("c", "beside"),
+    ("p", "by_done", 3), ("p", "az", 4, -1), ("p", "by", 1, -1), ("c", "beside"), ("p", "bz", 2), ("p", "by", 2, -2),
+    ("c", "beside"), ("c", "beside"), ("c", "beside"), ("c", "beside"), ("c", "beside"), ("c", "beside"),
+    ("p", "az", 3, 0), ("c", "beside"), ("p", "by", 2, 1), ("c", "beside"), ("p", "by_done", 2), ("p", "az", 4, 1),
+    ("p", "az_done", -1), ("c", "beside"), ("c", "beside"), ("p", "az", 4, 2), ("p", "by", 2, -1), ("c", "beside"),
+    ("c", "beside"), ("c", "beside"), ("p", "by_done", -2), ("p", "bz", 3), ("p", "by", 1, 0), ("c", "beside"),
+    ("c", "beside"), ("c", "beside"), ("c", "beside"), ("p", "az", 4, 0), ("p", "az_done", 1), ("p", "ay"),
+    ("p", "by_done", 1), ("c", "beside"), ("p", "az_done", 2), ("p", "ay_across"), ("c", "beside"),
+    ("p", "by_done", -1), ("c", "beside"), ("c", "beside"), ("c", "beside"), ("p", "by", 2, 0), ("p", "bz", 4),
+    ("c", "beside"), ("c", "beside"), ("c", "beside"), ("c", "beside"), ("p", "az_done", 0), ("c", "beside"),
+    ("c", "beside"), ("c", "beside"), ("c", "beside"), ("c", "beside"), ("p", "by_done", 0),
+)
 PAIRS = 3 * 38
 
 
@@ -698,11 +671,11 @@
             pltpu.VMEM((WIDTH, TOK), BF),
             pltpu.VMEM((2, 4, NY, CUT_P, WIDTH), BF),
             pltpu.VMEM((2, 2, NZ, rest, WIDTH), BF),
-            pltpu.VMEM((2, 2, CUT_P, WIDTH), BF),
+            pltpu.VMEM((3, CUT_P, WIDTH), BF),
             pltpu.VMEM((2, 4, rest, WIDTH), BF),
             pltpu.VMEM((TOK, WIDTH), BF),
             pltpu.VMEM((TOK, WIDTH), BF),
-            pltpu.SemaphoreType.DMA((16,)),
+            pltpu.SemaphoreType.DMA((18,)),
             pltpu.SemaphoreType.DMA((3,)),
             pltpu.SemaphoreType.DMA((PAIRS,)),
         ],

time: 107 us -> 97 us (0.907)
  Pallas kernels: 98.5 us -> 88.2 us
    pallas_call x1, Pallas kernels: 98.5 us -> 88.2 us  [backward(): pl.pallas_call(kernel, out_shape=(jax.ShapeDtypeStruct((1, TOK, WIDTH), B...]
where the time goes in v3:
time: 97 us; the launch traced here: 96.9 us
  Pallas kernels  88.2 us (91%)
  local copies, waits for them, and re-layouts  6.74 us (7%)
  between operations  1.94 us (2%)
    pallas_call x1, Pallas kernels, backward(): pl.pallas_call(kernel, out_shape=(jax.ShapeDtypeStruct((1, TOK, WIDTH), B...  88.2 us
    unnamed x5, local copies, waits for them, and re-layouts  6.74 us

profile of v3, /device:TPU:1, one launch (start us, length us, event | category | flops | bytes accessed | tf_op | source)
XLA Modules:
  0.0 96.9 jit_solution(3208302652685216631)
XLA Ops:
  1.9 88.2 %shard_map.130 = (bf16[1,256,256]{2,1,0:T(8,128)(2,1)}, bf16[1,320,4096]{2,1,0:T(8,128)(2,1)}, bf16[1,320,4096]{2,1,0:T(8,128)(2,1)}) custom-call(s32[1,320]{1,0:T(1,128)} %out_ids_hbm.1, s32[1,320]{1,0:T(1,128)} %val_ids_hbm.1, s32[1,1]{1,0:T(1,128)S(6)} %copy.17.out_count_hbm, s32[1,1]{1,0:T(1,128)S(6)} %copy.18.val_count_hbm, bf16[1,8192]{1,0:T(2,128)(2,1)} %gain_hbm.1, ...), custom_call_target="tpu_custom_call" | custom-call | flops 12884901888 | bytes 12582912 | tf_op jit(solution)/shard_map/pallas_call | solution.py:635
  90.1 1.6 %copy.19 = bf16[1,256,256]{2,1,0:T(8,128)(2,1)} copy(bf16[1,256,256]{2,1,0:T(8,128)(2,1)} %get-tuple-element.6) | data formatting | bytes 262144
  91.7 0.0 copy-start
  91.7 3.7 %copy.20 = bf16[1,320,4096]{2,1,0:T(8,128)(2,1)} copy(bf16[1,320,4096]{2,1,0:T(8,128)(2,1)} %get-tuple-element.7) | data formatting | bytes 5242880
  95.4 0.0 copy-done
  95.4 1.5 %copy.21 = bf16[1,320,4096]{2,1,0:T(8,128)(2,1)} copy(bf16[1,320,4096]{2,1,0:T(8,128)(2,1)S(1)} %copy-done) | data formatting | bytes 5242880
Async XLA Ops:
  91.7 3.7 %copy-start = (bf16[1,320,4096]{2,1,0:T(8,128)(2,1)S(1)}, bf16[1,320,4096]{2,1,0:T(8,128)(2,1)}, u32[]{:S(2)}) copy-start(bf16[1,320,4096]{2,1,0:T(8,128)(2,1)} %get-tuple-element.8) | copy-start | bytes 7864324
